TPU v7x, 32 devices: a whole 2x2x4 slice. The times are simulated.
32 devices in a mesh: lens: 2 (over y), gx: 16 (over z, x, core).
Axes of the slice: x: 2, y: 2, z: 4, core: 2. Of those that a mesh axis runs over, the one named last changes fastest.
Arguments:
- electric_init: float32 [3, 512, 24, 512], P(None, ('lens', 'gx')), parts along dimension 1, may hold values from -6 to 6
- magnetic_init: float32 [3, 512, 24, 512], P(None, ('lens', 'gx')), parts along dimension 1, may hold values from -6 to 6
- material: int32 [512, 24, 512], P(('lens', 'gx')), parts along dimension 0, may hold values from 0 to 3
- permittivity: float32 [8], P('lens'), parts along dimension 0, may hold values from 1 to 12
- monitor: int32 [2], P('lens'), parts along dimension 0, may hold values from 2 to 21
Outputs:
- electric: float32 [3, 512, 24, 512], P(None, ('lens', 'gx')), parts along dimension 1
- far_field: float32 [1024, 4, 2, 1024], P('gx', 'lens'), parts along dimension 1
There are 2 independent parts, one for each index of `lens`. A program takes and returns all parts, laid end to end along the dimension named above; each array names one. Nothing has to cross between parts.
Inputs may be any that keep to these rules, and one draw needn't show every extreme that they name: Each design's monitor plane lies inside the slab.
All inputs are finite; a program needn't handle non-finite values.
Results may differ from a plain program's by a relative error of at most 0.0001.
Values sent between devices are 32-bit elements; how exact they have to be, the bound alone decides.
A program may use at most 128 MiB of HBM per device.

v0:
```python
import functools
import math

import jax
import jax.numpy as jnp
import ml_dtypes
import numpy as np
from jax import lax
from jax.experimental import pallas as pl
from jax.experimental.pallas import tpu as pltpu
from jax.sharding import PartitionSpec as P

STEPS = 4
KX = 1024
KY = 1024
COURANT = 0.55
MESH = pl.DeviceIdType.MESH


def fdtd_kernel(
    n, e_in, h_in, mat_in, perm, mon, e_out, plane_out,
    E, H, CE, mat, low_e, low_h, up_e, G,
    load_sem, up_send, up_recv, dn_send, dn_recv, h0_send, h0_recv,
    ring_send, ring_recv, sib_send, sib_recv, out_sem,
):
    bx, nz, ny = E.shape[1:]
    me = lax.axis_index("gx")
    has_low, has_up = me > 0, me < n - 1
    chips = n // 2
    reach = chips // 2
    core, chip = me % 2, me // 2
    column, height = chip % 2, chip // 2
    place = height + column * (chips - 1 - 2 * height)

    def device_at(p, which):
        p = (p + 2 * chips) % chips
        back = p // reach
        at = (1 - back) * (2 * p) + back * (2 * (chips - 1 - p) + 1)
        return 2 * at + which

    ahead, behind = device_at(place + 1, core), device_at(place - 1, core)
    sibling = 2 * chip + (1 - core)

    barrier = pltpu.get_barrier_semaphore()

    def greet(other):
        pl.semaphore_signal(barrier, inc=1, device_id={"gx": other}, device_id_type=MESH)

    loads = [
        pltpu.make_async_copy(e_in, E, load_sem.at[0]),
        pltpu.make_async_copy(h_in, H, load_sem.at[1]),
        pltpu.make_async_copy(mat_in, mat, load_sem.at[2]),
    ]
    for other in (ahead, behind, sibling, (me + 1) % n, (me + n - 1) % n):
        greet(other)

    for load in (loads[2], loads[0], loads[1]):
        load.start()

    @pl.when(me == 0)
    def _():
        low_e[...] = jnp.zeros_like(low_e)
        low_h[...] = jnp.zeros_like(low_h)

    @pl.when(me == n - 1)
    def _():
        up_e[...] = jnp.zeros_like(up_e)

    pl.semaphore_wait(barrier, 5)

    def remote(src, dst, send, recv, other):
        return pltpu.make_async_remote_copy(
            src_ref=src, dst_ref=dst, send_sem=send, recv_sem=recv,
            device_id={"gx": other}, device_id_type=MESH,
        )

    def to_upper(r):
        src = e_in if r == 0 else E
        return remote(src.at[:, bx - 1], low_e.at[r], up_send.at[r], up_recv.at[r], me + 1)

    def to_lower(r):
        src = e_in if r == 0 else E
        return remote(src.at[1:3, 0], up_e.at[r], dn_send.at[r], dn_recv.at[r], me - 1)

    def first_h():
        return remote(h_in.at[1:3, bx - 1], low_h, h0_send, h0_recv, me + 1)

    @pl.when(has_up)
    def _():
        to_upper(0).start()
        first_h().start()

    @pl.when(has_low)
    def _():
        to_lower(0).start()

    lane = lax.broadcasted_iota(jnp.int32, (nz, ny), 1)
    row = lax.broadcasted_iota(jnp.int32, (nz, ny), 0)

    def next_y(v):
        return jnp.where(lane == ny - 1, 0.0, pltpu.roll(v, ny - 1, 1))

    def prev_y(v):
        return jnp.where(lane == 0, 0.0, pltpu.roll(v, 1, 1))

    def next_z(v):
        return jnp.where(row == nz - 1, 0.0, pltpu.roll(v, nz - 1, 0))

    def prev_z(v):
        return jnp.where(row == 0, 0.0, pltpu.roll(v, 1, 0))

    def step_h(x, ey_next, ez_next):
        ex, ey, ez = E[0, x], E[1, x], E[2, x]
        H[0, x] = H[0, x] - COURANT * ((next_y(ez) - ez) - (next_z(ey) - ey))
        H[1, x] = H[1, x] - COURANT * ((next_z(ex) - ex) - (ez_next - ez))
        H[2, x] = H[2, x] - COURANT * ((ey_next - ey) - (next_y(ex) - ex))

    def step_e(x, hy_prev, hz_prev):
        hx, hy, hz = H[0, x], H[1, x], H[2, x]
        ce = CE[x]
        E[0, x] = E[0, x] + ce * ((hz - prev_y(hz)) - (hy - prev_z(hy)))
        E[1, x] = E[1, x] + ce * ((hx - prev_z(hx)) - (hz - hz_prev))
        E[2, x] = E[2, x] + ce * ((hy - hy_prev) - (hx - prev_y(hx)))

    loads[2].wait()
    inverse = [COURANT * (1.0 / jnp.full((1, ny), perm[i], jnp.float32)) for i in range(perm.shape[0])]

    def coefficients(x, carry):
        index = mat[x]
        value = jnp.broadcast_to(inverse[-1], (nz, ny))
        for i in range(len(inverse) - 2, -1, -1):
            value = jnp.where(index == i, inverse[i], value)
        CE[x] = value
        return carry

    lax.fori_loop(0, bx, coefficients, 0)
    loads[0].wait()
    loads[1].wait()
    low_c = jnp.where(me > 0, COURANT, 0.0)

    def inner(x, carry):
        step_h(x, E[1, x + 1], E[2, x + 1])
        step_e(x, H[1, x - 1], H[2, x - 1])
        return carry

    for r in range(STEPS):
        step_h(0, E[1, 1], E[2, 1])
        lax.fori_loop(1, bx - 1, inner, 0)

        @pl.when(has_low)
        def _():
            to_lower(r).wait_send()
            to_upper(r).wait_recv()
            if r == 0:
                first_h().wait_recv()

        @pl.when(has_up)
        def _():
            to_upper(r).wait_send()
            if r == 0:
                first_h().wait_send()

        ex, ey, ez = low_e[r, 0], low_e[r, 1], low_e[r, 2]
        hy = low_h[0] - low_c * ((next_z(ex) - ex) - (E[2, 0] - ez))
        hz = low_h[1] - low_c * ((E[1, 0] - ey) - (next_y(ex) - ex))
        low_h[0] = hy
        low_h[1] = hz
        step_e(0, hy, hz)
        if r < STEPS - 1:

            @pl.when(has_low)
            def _():
                to_lower(r + 1).start()

        @pl.when(has_up)
        def _():
            to_lower(r).wait_recv()

        step_h(bx - 1, up_e[r, 0], up_e[r, 1])
        step_e(bx - 1, H[1, bx - 2], H[2, bx - 2])
        if r < STEPS - 1:

            @pl.when(has_up)
            def _():
                to_upper(r + 1).start()

    m = mon[0]
    for c in range(2):
        for x in range(bx):
            G[c, pl.ds(me * bx + x, 1), :] = E[c, x, pl.ds(m, 1), :]
    store = pltpu.make_async_copy(E, e_out, out_sem.at[0])

    def block(owner, c):
        return G.at[c, pl.ds(pl.multiple_of(owner * bx, bx), bx), :]

    def hop(way, s, c):
        owner = device_at(place - (s - 1), core) if way == 0 else device_at(place + (s - 1), core)
        ref = block(owner, c)
        return remote(
            ref, ref, ring_send.at[way, s - 1, c], ring_recv.at[way, s - 1, c], ahead if way == 0 else behind
        )

    def share(way, s, c):
        owner = device_at(place - s, core) if way == 0 else device_at(place + s, core)
        ref = block(owner, c)
        return remote(ref, ref, sib_send.at[way, s, c], sib_recv.at[way, s, c], sibling)

    hops = {(way, s, c) for way in range(2) for s in range(1, reach) for c in range(2)}
    hops |= {(0, reach, 0), (1, reach, 1)}
    for c in range(2):
        for way in range(2):
            if (way, 1, c) in hops:
                hop(way, 1, c).start()
    shares = [(0, 0, 0), (0, 0, 1)]
    for c in range(2):
        share(0, 0, c).start()
    store.start()
    for s in range(1, reach + 1):
        for c in range(2):
            for way in range(2):
                if (way, s, c) in hops:
                    hop(way, s, c).wait_recv()
                    if (way, s + 1, c) in hops:
                        hop(way, s + 1, c).start()
                    share(way, s, c).start()
                    shares.append((way, s, c))
    for item in shares:
        share(*item).wait_recv()
    keep = pltpu.make_async_copy(G, plane_out, out_sem.at[1])
    keep.start()
    for item in sorted(hops):
        hop(*item).wait_send()
    for item in shares:
        share(*item).wait_send()
    keep.wait()
    store.wait()


def split(value):
    high = value.astype(jnp.bfloat16)
    return high, (value - high.astype(jnp.float32)).astype(jnp.bfloat16)


def dot3(a_hi, a_lo, b_hi, b_lo):
    dot = functools.partial(jnp.dot, preferred_element_type=jnp.float32)
    return dot(a_hi, b_hi) + (dot(a_hi, b_lo) + dot(a_lo, b_hi))


def far_kernel(which, plane, x_hi, x_lo, y_hi, y_lo, e_in, e_out, far, l_hi, l_lo, sem):
    step = pl.program_id(0)
    rows = far.shape[0] * 2
    ny = plane.shape[2]
    copy = pltpu.make_async_copy(e_in, e_out, sem)

    @pl.when(step == 0)
    def _():
        copy.start()
        for c in range(2):
            p_hi, p_lo = split(plane[c])
            both = dot3(x_hi[0], x_lo[0], p_hi, p_lo)
            for part in range(2):
                high, low = split(both[part * rows : (part + 1) * rows])
                l_hi[c * rows : (c + 1) * rows, part * ny : (part + 1) * ny] = high
                l_lo[c * rows : (c + 1) * rows, part * ny : (part + 1) * ny] = low

    out = dot3(l_hi[...], l_lo[...], y_hi[...], y_lo[...])
    for c in range(2):
        far[:, c, :, :] = out[c * rows : (c + 1) * rows].reshape(rows // 2, 2, out.shape[1])

    @pl.when(step == pl.num_programs(0) - 1)
    def _():
        copy.wait()


def angles(count, positions):
    slope = 2 * np.arange(count, dtype=np.int64) + 1 - count
    turns = np.mod(slope[:, None] * np.arange(positions, dtype=np.int64)[None, :], 2 * count)
    return turns * (math.pi / count)


def halves(table):
    table = table.astype(np.float32)
    high = table.astype(ml_dtypes.bfloat16)
    return high, (table - high.astype(np.float32)).astype(ml_dtypes.bfloat16)


def tables(groups, full_x, width_y):
    scale = 1.0 / math.sqrt(full_x * width_y)
    angle_x = angles(KX, full_x).reshape(groups, KX // groups, full_x)
    cos_x, sin_x = scale * np.cos(angle_x), scale * np.sin(angle_x)
    shape = (groups, 2 * KX // groups, full_x)
    with_cos = np.stack([cos_x, -sin_x], axis=2).reshape(shape)
    with_sin = np.stack([-sin_x, -cos_x], axis=2).reshape(shape)
    angle_y = angles(KY, width_y)
    return halves(np.concatenate([with_cos, with_sin], axis=1)) + halves(
        np.concatenate([np.cos(angle_y).T, np.sin(angle_y).T], axis=0)
    )


def per_device(groups, electric_init, magnetic_init, material, permittivity, monitor):
    _, bx, nz, ny = electric_init.shape
    full_x = bx * groups
    reach = groups // 4
    f32 = jnp.float32
    anywhere = pl.BlockSpec(memory_space=pl.ANY)
    scalars = pl.BlockSpec(memory_space=pltpu.SMEM)
    dma = pltpu.SemaphoreType.DMA
    elec, plane = pl.pallas_call(
        functools.partial(fdtd_kernel, groups),
        out_shape=(
            jax.ShapeDtypeStruct(electric_init.shape, f32),
            jax.ShapeDtypeStruct((2, full_x, ny), f32),
        ),
        in_specs=[anywhere, anywhere, anywhere, scalars, scalars],
        out_specs=(anywhere, anywhere),
        scratch_shapes=[
            pltpu.VMEM((3, bx, nz, ny), f32),
            pltpu.VMEM((3, bx, nz, ny), f32),
            pltpu.VMEM((bx, nz, ny), f32),
            pltpu.VMEM((bx, nz, ny), jnp.int32),
            pltpu.VMEM((STEPS, 3, nz, ny), f32),
            pltpu.VMEM((2, nz, ny), f32),
            pltpu.VMEM((STEPS, 2, nz, ny), f32),
            pltpu.VMEM((2, full_x, ny), f32),
            dma((3,)),
            dma((STEPS,)),
            dma((STEPS,)),
            dma((STEPS,)),
            dma((STEPS,)),
            dma,
            dma,
            dma((2, reach, 2)),
            dma((2, reach, 2)),
            dma((2, reach + 1, 2)),
            dma((2, reach + 1, 2)),
            dma((2,)),
        ],
        compiler_params=pltpu.CompilerParams(
            collective_id=0, has_side_effects=True, vmem_limit_bytes=40 * 1024 * 1024
        ),
    )(electric_init, magnetic_init, material, permittivity, monitor)

    x_hi, x_lo, y_hi, y_lo = [jnp.asarray(table) for table in tables(groups, full_x, ny)]
    own = KX // groups
    tile = 256
    which = lax.axis_index("gx").astype(jnp.int32).reshape(1)
    electric, far_field = pl.pallas_call(
        far_kernel,
        out_shape=(
            jax.ShapeDtypeStruct(electric_init.shape, f32),
            jax.ShapeDtypeStruct((own, 2, 2, KY), f32),
        ),
        grid_spec=pltpu.PrefetchScalarGridSpec(
            num_scalar_prefetch=1,
            grid=(KY // tile,),
            in_specs=[
                pl.BlockSpec((2, full_x, ny), lambda j, w: (0, 0, 0)),
                pl.BlockSpec((1, 4 * own, full_x), lambda j, w: (w[0], 0, 0)),
                pl.BlockSpec((1, 4 * own, full_x), lambda j, w: (w[0], 0, 0)),
                pl.BlockSpec((2 * ny, tile), lambda j, w: (0, j)),
                pl.BlockSpec((2 * ny, tile), lambda j, w: (0, j)),
                anywhere,
            ],
            out_specs=(
                anywhere,
                pl.BlockSpec((own, 2, 2, tile), lambda j, w: (0, 0, 0, j)),
            ),
            scratch_shapes=[
                pltpu.VMEM((4 * own, 2 * ny), jnp.bfloat16),
                pltpu.VMEM((4 * own, 2 * ny), jnp.bfloat16),
                dma,
            ],
        ),
        compiler_params=pltpu.CompilerParams(vmem_limit_bytes=48 * 1024 * 1024),
    )(which, plane, x_hi, x_lo, y_hi, y_lo, elec)
    return electric, far_field


def solution(mesh):
    return jax.shard_map(
        functools.partial(per_device, mesh.shape["gx"]),
        mesh=mesh,
        in_specs=(
            P(None, ("lens", "gx"), None, None),
            P(None, ("lens", "gx"), None, None),
            P(("lens", "gx"), None, None),
            P("lens"),
            P("lens"),
        ),
        out_specs=(P(None, ("lens", "gx"), None, None), P("gx", "lens", None, None)),
        check_vma=False,
    )
```

profile of v0, /device:TPU:1, one launch (start us, length us, event | category | flops | bytes accessed | tf_op | source)
XLA Modules:
  0.0 119.7 jit_solution(4014550206715786504)
XLA Ops:
  1.3 0.0 copy-start
  1.3 1.7 %copy-done = f32[3,16,24,512]{3,2,1,0:T(8,128)S(1)} copy-done((f32[3,16,24,512]{3,2,1,0:T(8,128)S(1)}, f32[3,16,24,512]{3,2,1,0:T(8,128)}, u32[]{:S(2)}) %copy-start) | copy-done | bytes 2359320
  2.9 0.0 copy-start.1
  2.9 1.7 %copy-done.1 = f32[3,16,24,512]{3,2,1,0:T(8,128)S(1)} copy-done((f32[3,16,24,512]{3,2,1,0:T(8,128)S(1)}, f32[3,16,24,512]{3,2,1,0:T(8,128)}, u32[]{:S(2)}) %copy-start.1) | copy-done | bytes 2359320
  4.6 0.0 copy-start.5
  4.6 1.1 copy-done.5
  5.7 0.0 copy-start.6
  5.7 0.7 copy-done.6
  6.4 0.0 copy-start.3
  6.4 0.0 copy-start.4
  6.4 37.4 %shard_map.104 = (f32[3,16,24,512]{3,2,1,0:T(8,128)S(1)}, f32[2,256,512]{2,1,0:T(8,128)S(1)}) custom-call(f32[3,16,24,512]{3,2,1,0:T(8,128)S(1)} %copy-done, f32[3,16,24,512]{3,2,1,0:T(8,128)S(1)} %copy-done.1, s32[16,24,512]{2,1,0:T(8,128)S(1)} %copy-done.5, f32[4]{0:T(128)S(1)} %copy-done.6, s32[1]{0:T(128)S(6)} %copy.11.mon), custom_call_target="tpu_custom_call" | custom-call | tf_op jit(solution)/shard_map/pallas_call | solution.py:308
  43.8 0.0 copy-start.2
  43.8 1.4 %copy-done.2 = f32[3,16,24,512]{3,2,1,0:T(8,128)} copy-done((f32[3,16,24,512]{3,2,1,0:T(8,128)}, f32[3,16,24,512]{3,2,1,0:T(8,128)S(1)}, u32[]{:S(2)}) %copy-start.2) | copy-done | bytes 2359320
  45.2 0.0 copy-done.3
  45.2 0.0 copy-done.4
  45.2 74.5 %shard_map.105 = (f32[3,16,24,512]{3,2,1,0:T(8,128)}, f32[64,2,2,1024]{3,2,1,0:T(2,128)}) custom-call(s32[1]{0:T(128)} %bitcast.which, f32[2,256,512]{2,1,0:T(8,128)S(1)} %get-tuple-element.4.plane, bf16[16,256,256]{2,1,0:T(8,128)(2,1)S(1)} %copy-done.4, bf16[16,256,256]{2,1,0:T(8,128)(2,1)S(1)} %copy-done.3, bf16[1024,1024]{1,0:T(8,128)(2,1)} %constant.14.clone.y_hi, ...), custom_call_target="tpu_custom_call" | custom-call | tf_op jit(solution)/shard_map/pallas_call | solution.py:347
Async XLA Ops:
  1.3 1.7 %copy-start = (f32[3,16,24,512]{3,2,1,0:T(8,128)S(1)}, f32[3,16,24,512]{3,2,1,0:T(8,128)}, u32[]{:S(2)}) copy-start(f32[3,16,24,512]{3,2,1,0:T(8,128)} %e_in.1) | copy-start | bytes 7077892
  2.9 1.7 %copy-start.1 = (f32[3,16,24,512]{3,2,1,0:T(8,128)S(1)}, f32[3,16,24,512]{3,2,1,0:T(8,128)}, u32[]{:S(2)}) copy-start(f32[3,16,24,512]{3,2,1,0:T(8,128)} %h_in.1) | copy-start | bytes 7077892
  4.6 1.1 copy-start.5
  5.7 0.7 copy-start.6
  6.4 38.8 %copy-start.3 = (bf16[16,256,256]{2,1,0:T(8,128)(2,1)S(1)}, bf16[16,256,256]{2,1,0:T(8,128)(2,1)}, u32[]{:S(2)}) copy-start(bf16[16,256,256]{2,1,0:T(8,128)(2,1)} %constant.13.clone.x_lo) | copy-start | bytes 6291460
  6.4 38.8 %copy-start.4 = (bf16[16,256,256]{2,1,0:T(8,128)(2,1)S(1)}, bf16[16,256,256]{2,1,0:T(8,128)(2,1)}, u32[]{:S(2)}) copy-start(bf16[16,256,256]{2,1,0:T(8,128)(2,1)} %constant.12.clone.x_hi) | copy-start | bytes 6291460
  43.8 1.4 %copy-start.2 = (f32[3,16,24,512]{3,2,1,0:T(8,128)}, f32[3,16,24,512]{3,2,1,0:T(8,128)S(1)}, u32[]{:S(2)}) copy-start(f32[3,16,24,512]{3,2,1,0:T(8,128)S(1)} %get-tuple-element.5.e_in) | copy-start | bytes 7077892
where the time goes:
time: 120 us
  Pallas kernels  112 us (93%)
  local copies, waits for them, and re-layouts  6.51 us (5%)
  between operations  1.31 us (1%)
    pallas_call x1, Pallas kernels, per_device(): pl.pallas_call(far_kernel, out_shape=(jax.ShapeDtypeStruct(electric_init....  74.5 us
    pallas_call x1, Pallas kernels, per_device(): pl.pallas_call(functools.partial(fdtd_kernel, groups), out_shape=(jax.Sha...  37.4 us
    unnamed x14, local copies, waits for them, and re-layouts  6.51 us

commit v1 on v0

--- a/solution.py
+++ b/solution.py
@@ -18,28 +18,22 @@
 
 
 def fdtd_kernel(
-    n, e_in, h_in, mat_in, perm, mon, e_out, plane_out,
-    E, H, CE, mat, low_e, low_h, up_e, G,
+    n, e_in, h_in, mat_in, perm_in, mon, e_out, plane_out,
+    E, H, CE, mat, low_e, low_h, up_e, own, perm,
     load_sem, up_send, up_recv, dn_send, dn_recv, h0_send, h0_recv,
-    ring_send, ring_recv, sib_send, sib_recv, out_sem,
+    z_send, z_recv, x_send, x_recv, sib_send, sib_recv, out_sem,
 ):
     bx, nz, ny = E.shape[1:]
     me = lax.axis_index("gx")
     has_low, has_up = me > 0, me < n - 1
-    chips = n // 2
-    reach = chips // 2
-    core, chip = me % 2, me // 2
-    column, height = chip % 2, chip // 2
-    place = height + column * (chips - 1 - 2 * height)
-
-    def device_at(p, which):
-        p = (p + 2 * chips) % chips
-        back = p // reach
-        at = (1 - back) * (2 * p) + back * (2 * (chips - 1 - p) + 1)
-        return 2 * at + which
-
-    ahead, behind = device_at(place + 1, core), device_at(place - 1, core)
-    sibling = 2 * chip + (1 - core)
+    levels = n // 4
+    core, column, level = me % 2, (me // 2) % 2, me // 4
+
+    def device_at(z, x, c):
+        return 4 * ((z + levels) % levels) + 2 * x + c
+
+    mate = device_at(level, 1 - column, core)
+    sibling = device_at(level, column, 1 - core)
 
     barrier = pltpu.get_barrier_semaphore()
 
@@ -50,11 +44,13 @@
         pltpu.make_async_copy(e_in, E, load_sem.at[0]),
         pltpu.make_async_copy(h_in, H, load_sem.at[1]),
         pltpu.make_async_copy(mat_in, mat, load_sem.at[2]),
+        pltpu.make_async_copy(perm_in, perm, load_sem.at[3]),
     ]
-    for other in (ahead, behind, sibling, (me + 1) % n, (me + n - 1) % n):
+    lines = [device_at(level + d, column, core) for d in range(1, levels)]
+    for other in [mate, sibling, (me + 1) % n, (me + n - 1) % n] + lines:
         greet(other)
 
-    for load in (loads[2], loads[0], loads[1]):
+    for load in (loads[3], loads[2], loads[0], loads[1]):
         load.start()
 
     @pl.when(me == 0)
@@ -66,7 +62,7 @@
     def _():
         up_e[...] = jnp.zeros_like(up_e)
 
-    pl.semaphore_wait(barrier, 5)
+    pl.semaphore_wait(barrier, levels + 3)
 
     def remote(src, dst, send, recv, other):
         return pltpu.make_async_remote_copy(
@@ -109,20 +105,36 @@
     def prev_z(v):
         return jnp.where(row == 0, 0.0, pltpu.roll(v, 1, 0))
 
-    def step_h(x, ey_next, ez_next):
+    def new_h(x, ey_next, ez_next):
         ex, ey, ez = E[0, x], E[1, x], E[2, x]
-        H[0, x] = H[0, x] - COURANT * ((next_y(ez) - ez) - (next_z(ey) - ey))
-        H[1, x] = H[1, x] - COURANT * ((next_z(ex) - ex) - (ez_next - ez))
-        H[2, x] = H[2, x] - COURANT * ((ey_next - ey) - (next_y(ex) - ex))
-
-    def step_e(x, hy_prev, hz_prev):
+        return (
+            H[0, x] - COURANT * ((next_y(ez) - ez) - (next_z(ey) - ey)),
+            H[1, x] - COURANT * ((next_z(ex) - ex) - (ez_next - ez)),
+            H[2, x] - COURANT * ((ey_next - ey) - (next_y(ex) - ex)),
+        )
+
+    def new_e(x, hy_prev, hz_prev):
         hx, hy, hz = H[0, x], H[1, x], H[2, x]
         ce = CE[x]
-        E[0, x] = E[0, x] + ce * ((hz - prev_y(hz)) - (hy - prev_z(hy)))
-        E[1, x] = E[1, x] + ce * ((hx - prev_z(hx)) - (hz - hz_prev))
-        E[2, x] = E[2, x] + ce * ((hy - hy_prev) - (hx - prev_y(hx)))
-
-    loads[2].wait()
+        return (
+            E[0, x] + ce * ((hz - prev_y(hz)) - (hy - prev_z(hy))),
+            E[1, x] + ce * ((hx - prev_z(hx)) - (hz - hz_prev)),
+            E[2, x] + ce * ((hy - hy_prev) - (hx - prev_y(hx))),
+        )
+
+    def put(ref, x, values):
+        for c in range(3):
+            ref[c, x] = values[c]
+
+    def step_h(x, ey_next, ez_next):
+        put(H, x, new_h(x, ey_next, ez_next))
+
+    def step_e(x, hy_prev, hz_prev):
+        put(E, x, new_e(x, hy_prev, hz_prev))
+
+    for i in (3, 2):
+        loads[i].wait()
+    m = mon[0]
     inverse = [COURANT * (1.0 / jnp.full((1, ny), perm[i], jnp.float32)) for i in range(perm.shape[0])]
 
     def coefficients(x, carry):
@@ -139,13 +151,48 @@
     low_c = jnp.where(me > 0, COURANT, 0.0)
 
     def inner(x, carry):
+        ahead = new_h(x + 1, E[1, x + 2], E[2, x + 2])
+        here = new_e(x, H[1, x - 1], H[2, x - 1])
+        put(H, x + 1, ahead)
+        put(E, x, here)
+        return carry
+
+    def inner_h(x, carry):
         step_h(x, E[1, x + 1], E[2, x + 1])
+        return carry
+
+    def inner_e(x, carry):
         step_e(x, H[1, x - 1], H[2, x - 1])
         return carry
 
+    def block(owner):
+        return plane_out.at[:, pl.ds(pl.multiple_of(owner * bx, bx), bx), :]
+
+    def along(d):
+        return remote(own, block(me), z_send.at[d], z_recv.at[d], device_at(level + d, column, core))
+
+    def across(d):
+        owner = device_at(level - d, column, core)
+        return remote(own if d == 0 else block(owner), block(owner), x_send.at[d], x_recv.at[d], mate)
+
+    def share(side, d):
+        owner = device_at(level - d, column + side * (1 - 2 * column), core)
+        src = own if side == 0 and d == 0 else block(owner)
+        return remote(src, block(owner), sib_send.at[side, d], sib_recv.at[side, d], sibling)
+
+    order = sorted(range(1, levels), key=lambda d: (min(d, levels - d), d))
+    store = pltpu.make_async_copy(E, e_out, out_sem.at[0])
+    keep = pltpu.make_async_copy(own, block(me), out_sem.at[1])
+
     for r in range(STEPS):
-        step_h(0, E[1, 1], E[2, 1])
-        lax.fori_loop(1, bx - 1, inner, 0)
+        last = r == STEPS - 1
+        if last:
+            lax.fori_loop(0, bx - 1, inner_h, 0)
+        else:
+            step_h(0, E[1, 1], E[2, 1])
+            step_h(1, E[1, 2], E[2, 2])
+            lax.fori_loop(1, bx - 2, inner, 0)
+            step_e(bx - 2, H[1, bx - 3], H[2, bx - 3])
 
         @pl.when(has_low)
         def _():
@@ -165,8 +212,8 @@
         hz = low_h[1] - low_c * ((E[1, 0] - ey) - (next_y(ex) - ex))
         low_h[0] = hy
         low_h[1] = hz
-        step_e(0, hy, hz)
-        if r < STEPS - 1:
+        if not last:
+            step_e(0, hy, hz)
 
             @pl.when(has_low)
             def _():
@@ -177,61 +224,50 @@
             to_lower(r).wait_recv()
 
         step_h(bx - 1, up_e[r, 0], up_e[r, 1])
-        step_e(bx - 1, H[1, bx - 2], H[2, bx - 2])
-        if r < STEPS - 1:
+        if not last:
+            step_e(bx - 1, H[1, bx - 2], H[2, bx - 2])
 
             @pl.when(has_up)
             def _():
                 to_upper(r + 1).start()
 
-    m = mon[0]
-    for c in range(2):
-        for x in range(bx):
-            G[c, pl.ds(me * bx + x, 1), :] = E[c, x, pl.ds(m, 1), :]
-    store = pltpu.make_async_copy(E, e_out, out_sem.at[0])
-
-    def block(owner, c):
-        return G.at[c, pl.ds(pl.multiple_of(owner * bx, bx), bx), :]
-
-    def hop(way, s, c):
-        owner = device_at(place - (s - 1), core) if way == 0 else device_at(place + (s - 1), core)
-        ref = block(owner, c)
-        return remote(
-            ref, ref, ring_send.at[way, s - 1, c], ring_recv.at[way, s - 1, c], ahead if way == 0 else behind
-        )
-
-    def share(way, s, c):
-        owner = device_at(place - s, core) if way == 0 else device_at(place + s, core)
-        ref = block(owner, c)
-        return remote(ref, ref, sib_send.at[way, s, c], sib_recv.at[way, s, c], sibling)
-
-    hops = {(way, s, c) for way in range(2) for s in range(1, reach) for c in range(2)}
-    hops |= {(0, reach, 0), (1, reach, 1)}
-    for c in range(2):
-        for way in range(2):
-            if (way, 1, c) in hops:
-                hop(way, 1, c).start()
-    shares = [(0, 0, 0), (0, 0, 1)]
-    for c in range(2):
-        share(0, 0, c).start()
+    first = lax.broadcasted_iota(jnp.int32, (1, ny), 1) == 0
+    at, under = pl.ds(m, 1), pl.ds(jnp.maximum(m - 1, 0), 1)
+    for x in range(bx):
+        hx, hy, hz = [H[c, x, at, :] for c in range(3)]
+        hz_prev = low_h[1, at, :] if x == 0 else H[2, x - 1, at, :]
+        ce = CE[x, at, :]
+        side = jnp.where(first, 0.0, pltpu.roll(hz, 1, 1))
+        own[0, x : x + 1, :] = E[0, x, at, :] + ce * ((hz - side) - (hy - H[1, x, under, :]))
+        own[1, x : x + 1, :] = E[1, x, at, :] + ce * ((hx - H[0, x, under, :]) - (hz - hz_prev))
+
+    across(0).start()
+    for d in order[::-1]:
+        along(d).start()
+    share(0, 0).start()
+    keep.start()
+    step_e(0, low_h[0], low_h[1])
+    lax.fori_loop(1, bx, inner_e, 0)
     store.start()
-    for s in range(1, reach + 1):
-        for c in range(2):
-            for way in range(2):
-                if (way, s, c) in hops:
-                    hop(way, s, c).wait_recv()
-                    if (way, s + 1, c) in hops:
-                        hop(way, s + 1, c).start()
-                    share(way, s, c).start()
-                    shares.append((way, s, c))
-    for item in shares:
-        share(*item).wait_recv()
-    keep = pltpu.make_async_copy(G, plane_out, out_sem.at[1])
-    keep.start()
-    for item in sorted(hops):
-        hop(*item).wait_send()
-    for item in shares:
-        share(*item).wait_send()
+
+    across(0).wait_recv()
+    share(1, 0).start()
+    for d in order:
+        along(d).wait_recv()
+        across(d).start()
+        share(0, d).start()
+    for d in order:
+        across(d).wait_recv()
+        share(1, d).start()
+    for d in [0] + order:
+        share(0, d).wait_recv()
+        share(1, d).wait_recv()
+    for d in [0] + order:
+        if d > 0:
+            along(d).wait_send()
+        across(d).wait_send()
+        share(0, d).wait_send()
+        share(1, d).wait_send()
     keep.wait()
     store.wait()
 
@@ -300,10 +336,14 @@
 def per_device(groups, electric_init, magnetic_init, material, permittivity, monitor):
     _, bx, nz, ny = electric_init.shape
     full_x = bx * groups
-    reach = groups // 4
+    levels = groups // 4
     f32 = jnp.float32
     anywhere = pl.BlockSpec(memory_space=pl.ANY)
-    scalars = pl.BlockSpec(memory_space=pltpu.SMEM)
+
+    def in_hbm(value):
+        return pltpu.with_memory_space_constraint(value, pltpu.HBM)
+
+    off_core = pl.BlockSpec(memory_space=pltpu.HBM)
     dma = pltpu.SemaphoreType.DMA
     elec, plane = pl.pallas_call(
         functools.partial(fdtd_kernel, groups),
@@ -311,7 +351,7 @@
             jax.ShapeDtypeStruct(electric_init.shape, f32),
             jax.ShapeDtypeStruct((2, full_x, ny), f32),
         ),
-        in_specs=[anywhere, anywhere, anywhere, scalars, scalars],
+        in_specs=[off_core] * 4 + [pl.BlockSpec(memory_space=pltpu.SMEM)],
         out_specs=(anywhere, anywhere),
         scratch_shapes=[
             pltpu.VMEM((3, bx, nz, ny), f32),
@@ -321,26 +361,29 @@
             pltpu.VMEM((STEPS, 3, nz, ny), f32),
             pltpu.VMEM((2, nz, ny), f32),
             pltpu.VMEM((STEPS, 2, nz, ny), f32),
-            pltpu.VMEM((2, full_x, ny), f32),
-            dma((3,)),
+            pltpu.VMEM((2, bx, ny), f32),
+            pltpu.SMEM(permittivity.shape, f32),
+            dma((4,)),
             dma((STEPS,)),
             dma((STEPS,)),
             dma((STEPS,)),
             dma((STEPS,)),
             dma,
             dma,
-            dma((2, reach, 2)),
-            dma((2, reach, 2)),
-            dma((2, reach + 1, 2)),
-            dma((2, reach + 1, 2)),
+            dma((levels,)),
+            dma((levels,)),
+            dma((levels,)),
+            dma((levels,)),
+            dma((2, levels)),
+            dma((2, levels)),
             dma((2,)),
         ],
         compiler_params=pltpu.CompilerParams(
-            collective_id=0, has_side_effects=True, vmem_limit_bytes=40 * 1024 * 1024
+            collective_id=0, has_side_effects=True, vmem_limit_bytes=24 * 1024 * 1024
         ),
-    )(electric_init, magnetic_init, material, permittivity, monitor)
-
-    x_hi, x_lo, y_hi, y_lo = [jnp.asarray(table) for table in tables(groups, full_x, ny)]
+    )(*map(in_hbm, (electric_init, magnetic_init, material, permittivity)), monitor)
+
+    x_hi, x_lo, y_hi, y_lo = [in_hbm(jnp.asarray(table)) for table in tables(groups, full_x, ny)]
     own = KX // groups
     tile = 256
     which = lax.axis_index("gx").astype(jnp.int32).reshape(1)
@@ -371,7 +414,7 @@
                 dma,
             ],
         ),
-        compiler_params=pltpu.CompilerParams(vmem_limit_bytes=48 * 1024 * 1024),
+        compiler_params=pltpu.CompilerParams(vmem_limit_bytes=28 * 1024 * 1024),
     )(which, plane, x_hi, x_lo, y_hi, y_lo, elec)
     return electric, far_field
 

time: 120 us -> 42.6 us (0.36)
  Pallas kernels: 112 us -> 40.6 us
  local copies, waits for them, and re-layouts: 6.51 us -> 0 us
    pallas_call x1, Pallas kernels: 74.5 us -> 5.78 us  [per_device(): pl.pallas_call(far_kernel, out_shape=(jax.ShapeDtypeStruct(electric_init....]
    unnamed x14 -> x0, local copies, waits for them, and re-layouts: 6.51 us -> none
    pallas_call x1, Pallas kernels: 37.4 us -> 34.8 us  [per_device(): pl.pallas_call(functools.partial(fdtd_kernel, groups), out_shape=(jax.Sha...]
where the time goes in v1:
time: 42.6 us; the launch traced here: 41.9 us
  Pallas kernels  40.6 us (95%)
  between operations  1.29 us (3%)
    pallas_call x1, Pallas kernels, per_device(): pl.pallas_call(functools.partial(fdtd_kernel, groups), out_shape=(jax.Sha...  34.8 us
    pallas_call x1, Pallas kernels, per_device(): pl.pallas_call(far_kernel, out_shape=(jax.ShapeDtypeStruct(electric_init....  5.78 us

profile of v1, /device:TPU:1, one launch (start us, length us, event | category | flops | bytes accessed | tf_op | source)
XLA Modules:
  0.0 41.9 jit_solution(581997424305572049)
XLA Ops:
  1.3 34.8 %shard_map.104 = (f32[3,16,24,512]{3,2,1,0:T(8,128)S(1)}, f32[2,256,512]{2,1,0:T(8,128)S(1)}) custom-call(f32[3,16,24,512]{3,2,1,0:T(8,128)} %e_in.1, f32[3,16,24,512]{3,2,1,0:T(8,128)} %h_in.1, s32[16,24,512]{2,1,0:T(8,128)} %mat_in.1, f32[4]{0:T(128)} %perm_in.1, s32[1]{0:T(128)S(6)} %copy.11.mon), custom_call_target="tpu_custom_call" | custom-call | tf_op jit(solution)/shard_map/pallas_call | solution.py:348
  36.1 5.8 %shard_map.105 = (f32[3,16,24,512]{3,2,1,0:T(8,128)}, f32[64,2,2,1024]{3,2,1,0:T(2,128)}) custom-call(s32[1]{0:T(128)} %bitcast.which, f32[2,256,512]{2,1,0:T(8,128)S(1)} %get-tuple-element.4.plane, bf16[16,256,256]{2,1,0:T(8,128)(2,1)} %constant.12.clone.x_hi, bf16[16,256,256]{2,1,0:T(8,128)(2,1)} %constant.13.clone.x_lo, ...), custom_call_target="tpu_custom_call" | custom-call | tf_op jit(solution)/shard_map/pallas_call | solution.py:390

commit v2 on v1

--- a/solution.py
+++ b/solution.py
@@ -18,7 +18,8 @@
 
 
 def fdtd_kernel(
-    n, e_in, h_in, mat_in, perm_in, mon, e_out, plane_out,
+    n, e_in, h_in, mat_in, perm_in, mon, y_hi, y_lo,
+    e_out, plane_out, y_hi_out, y_lo_out,
     E, H, CE, mat, low_e, low_h, up_e, own, perm,
     load_sem, up_send, up_recv, dn_send, dn_recv, h0_send, h0_recv,
     z_send, z_recv, x_send, x_recv, sib_send, sib_recv, out_sem,
@@ -45,6 +46,8 @@
         pltpu.make_async_copy(h_in, H, load_sem.at[1]),
         pltpu.make_async_copy(mat_in, mat, load_sem.at[2]),
         pltpu.make_async_copy(perm_in, perm, load_sem.at[3]),
+        pltpu.make_async_copy(y_hi, y_hi_out, load_sem.at[4]),
+        pltpu.make_async_copy(y_lo, y_lo_out, load_sem.at[5]),
     ]
     lines = [device_at(level + d, column, core) for d in range(1, levels)]
     for other in [mate, sibling, (me + 1) % n, (me + n - 1) % n] + lines:
@@ -148,6 +151,8 @@
     lax.fori_loop(0, bx, coefficients, 0)
     loads[0].wait()
     loads[1].wait()
+    loads[4].start()
+    loads[5].start()
     low_c = jnp.where(me > 0, COURANT, 0.0)
 
     def inner(x, carry):
@@ -270,6 +275,8 @@
         share(1, d).wait_send()
     keep.wait()
     store.wait()
+    loads[4].wait()
+    loads[5].wait()
 
 
 def split(value):
@@ -345,14 +352,17 @@
 
     off_core = pl.BlockSpec(memory_space=pltpu.HBM)
     dma = pltpu.SemaphoreType.DMA
-    elec, plane = pl.pallas_call(
+    x_hi, x_lo, y_hi, y_lo = [in_hbm(jnp.asarray(table)) for table in tables(groups, full_x, ny)]
+    elec, plane, y_hi, y_lo = pl.pallas_call(
         functools.partial(fdtd_kernel, groups),
         out_shape=(
             jax.ShapeDtypeStruct(electric_init.shape, f32),
             jax.ShapeDtypeStruct((2, full_x, ny), f32),
+            jax.ShapeDtypeStruct(y_hi.shape, y_hi.dtype),
+            jax.ShapeDtypeStruct(y_lo.shape, y_lo.dtype),
         ),
-        in_specs=[off_core] * 4 + [pl.BlockSpec(memory_space=pltpu.SMEM)],
-        out_specs=(anywhere, anywhere),
+        in_specs=[off_core] * 4 + [pl.BlockSpec(memory_space=pltpu.SMEM)] + [off_core] * 2,
+        out_specs=(anywhere,) * 4,
         scratch_shapes=[
             pltpu.VMEM((3, bx, nz, ny), f32),
             pltpu.VMEM((3, bx, nz, ny), f32),
@@ -363,7 +373,7 @@
             pltpu.VMEM((STEPS, 2, nz, ny), f32),
             pltpu.VMEM((2, bx, ny), f32),
             pltpu.SMEM(permittivity.shape, f32),
-            dma((4,)),
+            dma((6,)),
             dma((STEPS,)),
             dma((STEPS,)),
             dma((STEPS,)),
@@ -381,9 +391,8 @@
         compiler_params=pltpu.CompilerParams(
             collective_id=0, has_side_effects=True, vmem_limit_bytes=24 * 1024 * 1024
         ),
-    )(*map(in_hbm, (electric_init, magnetic_init, material, permittivity)), monitor)
-
-    x_hi, x_lo, y_hi, y_lo = [in_hbm(jnp.asarray(table)) for table in tables(groups, full_x, ny)]
+    )(*map(in_hbm, (electric_init, magnetic_init, material, permittivity)), monitor, y_hi, y_lo)
+
     own = KX // groups
     tile = 256
     which = lax.axis_index("gx").astype(jnp.int32).reshape(1)

time: 42.6 us -> 42 us (0.986)
  Pallas kernels: 40.6 us -> 40 us
    pallas_call x1, Pallas kernels: 5.78 us -> 5.13 us  [per_device(): pl.pallas_call(far_kernel, out_shape=(jax.ShapeDtypeStruct(electric_init....]
where the time goes in v2:
time: 42 us; the launch traced here: 41.2 us
  Pallas kernels  40 us (95%)
  between operations  1.29 us (3%)
    pallas_call x1, Pallas kernels, per_device(): pl.pallas_call(functools.partial(fdtd_kernel, groups), out_shape=(jax.Sha...  34.8 us
    pallas_call x1, Pallas kernels, per_device(): pl.pallas_call(far_kernel, out_shape=(jax.ShapeDtypeStruct(electric_init....  5.13 us

profile of v2, /device:TPU:1, one launch (start us, length us, event | category | flops | bytes accessed | tf_op | source)
XLA Modules:
  0.0 41.2 jit_solution(5672525703106915495)
XLA Ops:
  1.3 34.8 %shard_map.104 = (f32[3,16,24,512]{3,2,1,0:T(8,128)S(1)}, f32[2,256,512]{2,1,0:T(8,128)S(1)}, bf16[1024,1024]{1,0:T(8,128)(2,1)S(1)}, bf16[1024,1024]{1,0:T(8,128)(2,1)S(1)}) custom-call(f32[3,16,24,512]{3,2,1,0:T(8,128)} %e_in.1, f32[3,16,24,512]{3,2,1,0:T(8,128)} %h_in.1, s32[16,24,512]{2,1,0:T(8,128)} %mat_in.1, f32[4]{0:T(128)} %perm_in.1, ...), custom_call_target="tpu_custom_call" | custom-call | tf_op jit(solution)/shard_map/pallas_call | solution.py:356
  36.1 5.1 %shard_map.105 = (f32[3,16,24,512]{3,2,1,0:T(8,128)}, f32[64,2,2,1024]{3,2,1,0:T(2,128)}) custom-call(s32[1]{0:T(128)} %bitcast.which, f32[2,256,512]{2,1,0:T(8,128)S(1)} %get-tuple-element.6.plane, bf16[16,256,256]{2,1,0:T(8,128)(2,1)} %constant.12.clone.x_hi, bf16[16,256,256]{2,1,0:T(8,128)(2,1)} %constant.13.clone.x_lo, ...), custom_call_target="tpu_custom_call" | custom-call | tf_op jit(solution)/shard_map/pallas_call | solution.py:399
